TPU v7x, 32 devices: a whole 2x2x4 slice. The times are simulated.
32 devices in a mesh: inst: 2 (over x), cell: 16 (over z, y, core).
Axes of the slice: x: 2, y: 2, z: 4, core: 2. Of those that a mesh axis runs over, the one named last changes fastest.
Arguments:
- adjoint: float32 [16, 6, 16384], P('inst', None, 'cell'), may hold values from -6 to 6
- source: float32 [16, 6, 16384], P('inst', None, 'cell'), may hold values from -6 to 6
- jac_diag: bfloat16 [16, 6, 6, 16384], P('inst', None, None, 'cell'), may hold values from -6 to 6
- jac_face: bfloat16 [16, 4, 6, 6, 16384], P('inst', None, None, None, 'cell'), may hold values from -4 to 4
- tile_nbr: int32 [128, 4], P('cell'), may hold values from 0 to 7
- dtau: float32 [16384], P('cell'), may hold values from 0.1 to 0.5
- fringe_src: int32 [16, 16, 64], P('cell'), may hold values from 0 to 1023
- fringe_wt: float32 [16, 16, 64], P('cell'), may hold values from 0.2 to 1
- fringe_count: int32 [16, 16], P('cell'), may hold values from 0 to 64, as said below
- fringe_dst: int32 [16, 16, 64], P(None, 'cell'), may hold values from 0 to 1023
Outputs:
- updated: float32 [16, 6, 16384], P('inst', None, 'cell')
Inputs may be any that keep to these rules, and one draw needn't show every extreme that they name: `fringe_count`: each group sends 64 live slots to at least one donor owner; group loads differ by up to four times.
All inputs are finite; a program needn't handle non-finite values.
Results may differ from a plain program's by a relative error of at most 0.0003.
Values sent between devices are 32-bit elements; how exact they have to be, the bound alone decides.
A program may use at most 64 MiB of HBM per device.

v0:
```python
import math

import jax
import jax.numpy as jnp
from jax import lax
from jax.sharding import PartitionSpec as P

INSTANCES = 16
FACES = 4
TILE = 128


def spectral_matrix(count):
    rows = jnp.arange(count, dtype=jnp.int32)[:, None]
    cols = jnp.arange(count, dtype=jnp.int32)[None, :]
    offset = rows - cols
    angle = offset.astype(jnp.float32) * (jnp.pi / count)
    parity = jnp.where(offset % 2 == 0, 1.0, -1.0).astype(jnp.float32)
    denom = jnp.where(offset == 0, 1.0, jnp.sin(angle))
    value = 0.25 * parity * jnp.cos(angle) / denom
    return jnp.where(offset == 0, 0.0, value)


def pick_rows(flat, sources, weights, block):
    cells_dev = flat.shape[1]
    nblocks = sources.shape[0] // block
    cell_ids = jnp.arange(cells_dev, dtype=jnp.int32)[:, None]

    def one_block(pair):
        index_block, weight_block = pair
        select = jnp.where(cell_ids == index_block[None, :], weight_block[None, :], 0.0)
        return jnp.dot(
            flat, select, precision=lax.Precision.HIGHEST, preferred_element_type=jnp.float32
        )

    result = lax.map(one_block, (sources.reshape(nblocks, block), weights.reshape(nblocks, block)))
    return jnp.transpose(result, (1, 0, 2)).reshape(flat.shape[0], -1)


def place_rows(values, targets, cells_dev, block):
    nblocks = targets.shape[0] // block
    cell_ids = jnp.arange(cells_dev, dtype=jnp.int32)[None, :]

    def add_block(step, total):
        start = step * block
        target_block = lax.dynamic_slice_in_dim(targets, start, block, 0)
        value_block = lax.dynamic_slice_in_dim(values, start, block, 1)
        select = jnp.where(target_block[:, None] == cell_ids, 1.0, 0.0).astype(jnp.float32)
        return total + jnp.dot(
            value_block, select, precision=lax.Precision.HIGHEST, preferred_element_type=jnp.float32
        )

    empty = jnp.zeros((values.shape[0], cells_dev), jnp.float32)
    return lax.fori_loop(0, nblocks, add_block, empty)


def on_device(
    adjoint,
    source,
    jac_diag,
    jac_face,
    tile_nbr,
    dtau,
    fringe_src,
    fringe_wt,
    fringe_count,
    fringe_dst,
):
    inst_dev, nvars, cells_dev = adjoint.shape
    tiles_dev = cells_dev // TILE
    peer_count, slot_cap = (fringe_wt.shape[1], fringe_wt.shape[2])
    total_slots = peer_count * slot_cap
    block = math.gcd(total_slots, 512)
    smat = spectral_matrix(INSTANCES)
    flat = adjoint.reshape(inst_dev * nvars, cells_dev)
    live = jnp.arange(slot_cap, dtype=jnp.int32)[None, :] < fringe_count[0][:, None]
    coef = jnp.where(live, fringe_wt[0], 0.0).reshape(-1)
    picked = pick_rows(flat, fringe_src[0].reshape(-1), coef, block)
    outgoing = picked.reshape(inst_dev, nvars, peer_count, slot_cap)
    arrived = lax.all_to_all(outgoing, "cell", split_axis=2, concat_axis=2, tiled=True)
    spread = lax.all_to_all(adjoint, "inst", split_axis=2, concat_axis=0, tiled=True)
    mixed = jnp.einsum("ji,jac->iac", smat, spread, precision=lax.Precision.HIGHEST)
    temporal = lax.all_to_all(mixed, "inst", split_axis=0, concat_axis=2, tiled=True)
    own = jnp.sum(jac_diag.astype(jnp.float32) * adjoint[:, :, None, :], axis=1)
    tiles = adjoint.reshape(inst_dev, nvars, tiles_dev, TILE)
    tile_ids = jnp.arange(tiles_dev, dtype=jnp.int32)[None, :]
    faced = jnp.zeros_like(adjoint)
    for face in range(FACES):
        select = jnp.where(tile_nbr[:, face][:, None] == tile_ids, 1.0, 0.0).astype(jnp.float32)
        near = jnp.einsum("tu,iaup->iatp", select, tiles, precision=lax.Precision.HIGHEST)
        near = near.reshape(inst_dev, nvars, cells_dev)
        faced = faced + jnp.sum(jac_face[:, face].astype(jnp.float32) * near[:, :, None, :], axis=1)
    donors = fringe_dst[:, 0, :].reshape(-1)
    fringe = place_rows(arrived.reshape(inst_dev * nvars, -1), donors, cells_dev, block)
    fringe = fringe.reshape(inst_dev, nvars, cells_dev)
    total = own + faced + temporal + fringe - source
    return adjoint - dtau[None, None, :] * total


def solution(mesh):
    placed = (
        P("inst", None, "cell"),
        P("inst", None, "cell"),
        P("inst", None, None, "cell"),
        P("inst", None, None, None, "cell"),
        P("cell", None),
        P("cell"),
        P("cell", None, None),
        P("cell", None, None),
        P("cell", None),
        P(None, "cell", None),
    )
    return jax.shard_map(
        on_device, mesh=mesh, in_specs=placed, out_specs=P("inst", None, "cell"), check_vma=False
    )
```

profile of v0, /device:TPU:0, one launch (start us, length us, event | category | flops | bytes accessed | tf_op | source)
XLA Modules:
  0.0 66.9 jit_solution(3277994474411450989)
XLA Ops:
  0.0 3.4 %copy.103 = f32[8,6,1024]{0,1,2:T(8,128)} copy(f32[8,6,1024]{2,0,1:T(8,128)} %param.14) | data formatting | bytes 393216 | tf_op args[0]
  3.4 3.8 %reshape.64 = f32[2,1,24576]{2,1,0:T(1,128)} reshape(f32[1024,6,8]{2,1,0:T(8,128)} %bitcast.115) | data formatting | bytes 393216
  7.2 4.2 %all-to-all-start = ((f32[2,1,24576]{2,1,0:T(1,128)}), f32[2,1,24576]{2,1,0:T(1,128)S(1)}, u32[]{:S(2)}, u32[]{:S(2)}) async-start(f32[2,1,24576]{2,1,0:T(1,128)} %reshape.64), calls=%async_computation | async-start | bytes 393216 | tf_op jit(solution)/shard_map/all_to_all | solution.py:81
  12.4 6.2 %fusion.106 = (bf16[8,1,6,6,1024]{4,1,3,2,0:T(2,128)(2,1)}, bf16[8,1,6,6,1024]{4,1,3,2,0:T(2,128)(2,1)}, bf16[8,1,6,6,1024]{4,1,3,2,0:T(2,128)(2,1)}, bf16[8,1,6,6,1024]{4,1,3,2,0:T(2,128)(2,1)}) fusion(bf16[8,4,6,6,1024]{4,1,3,2,0:T(4,128)(2,1)S(1)} %copy-done.1), kind=kLoop, calls=%fused_computation.126 | loop fusion | bytes 4718592 | tf_op jit(solution)/shard_map/slice | solution.py:92
  18.6 0.6 broadcast.31
  19.2 0.7 %reduce.6 = s32[16]{0:T(128)S(1)} reduce(s32[1,16]{1,0:T(1,128)S(1)} %copy-done.19, s32[]{:T(128)} %broadcast.31), dimensions={0}, to_apply=%param.22.reduce_sub_computation.3 | reduce | bytes 132 | tf_op args[8]
  20.4 4.4 %while.25 = (s32[]{:T(128)}, f32[2,48,512]{2,1,0:T(8,128)}, s32[2,512]{1,0:T(2,128)S(1)}, f32[2,512]{1,0:T(2,128)S(1)}, f32[48,1024]{1,0:T(8,128)S(1)}, /*index=5*/s32[]{:T(128)}) while((s32[]{:T(128)}, f32[2,48,512]{2,1,0:T(8,128)}, s32[2,512]{1,0:T(2,128)S(1)}, f32[2,512]{1,0:T(2,128)S(1)}, f32[48,1024]{1,0:T(8,128)S(1)}, ...), condition=%wide.region_6.7_spmd.clone, body=%wide.region_5.6_spmd.clone.sunk | while | flops 303038464 | bytes 307789 | solution.py:36
  20.4 2.2 %fusion.116 = f32[2,48,512]{2,1,0:T(8,128)} fusion(f32[2,48,512]{2,1,0:T(8,128)} %get-tuple-element.255, s32[]{:T(128)} %get-tuple-element.254, f32[48,1024]{1,0:T(8,128)S(1)} %get-tuple-element.264, f32[512]{0:T(512)S(1)} %bitcast.124, s32[512]{0:T(512)S(1)} %bitcast.125), kind=kOutput, calls=%fused_computation.6.clone.1 | convolution fusion | flops 303038464 | bytes 299520 | tf_op jit(solution)/shard_map/while/body/eval_jaxpr/dot_general | solution.py:32
  22.6 2.2 %fusion.116 = f32[2,48,512]{2,1,0:T(8,128)} fusion(f32[2,48,512]{2,1,0:T(8,128)} %get-tuple-element.255, s32[]{:T(128)} %get-tuple-element.254, f32[48,1024]{1,0:T(8,128)S(1)} %get-tuple-element.264, f32[512]{0:T(512)S(1)} %bitcast.124, s32[512]{0:T(512)S(1)} %bitcast.125), kind=kOutput, calls=%fused_computation.6.clone.1 | convolution fusion | flops 303038464 | bytes 299520 | tf_op jit(solution)/shard_map/while/body/eval_jaxpr/dot_general | solution.py:32
  24.8 1.1 %convolution_bitcast_fusion.3 = f32[8,6,8,128]{3,2,1,0:T(8,128)} fusion(f32[8,6,8,128]{3,0,2,1:T(8,128)S(1)} %bitcast.118, s32[8]{0:T(128)S(1)} %get-tuple-element.185), kind=kOutput, calls=%fused_computation.36 | convolution fusion | flops 4718720 | bytes 393248 | tf_op jit(solution)/shard_map/tu,iaup->iatp/dot_general | solution.py:90
  25.9 0.6 broadcast.33
  26.4 1.2 %reduce.9 = f32[2,24576]{1,0:T(2,128)S(1)} reduce(f32[2,1,24576]{2,1,0:T(1,128)S(1)} %all-to-all-done, f32[]{:T(128)} %broadcast.33), dimensions={1}, to_apply=%all_to_all.29.reduce_sub_computation | reduce | bytes 393220 | tf_op jit(solution)/shard_map/all_to_all | solution.py:81
  27.7 3.8 %reshape.65 = f32[1024,6,8]{2,1,0:T(8,128)} reshape(f32[2,24576]{1,0:T(2,128)S(1)} %reduce.9) | data formatting | bytes 393216
  31.5 2.7 %copy.104 = f32[8,6,2,512]{3,0,2,1:T(8,128)S(1)} copy(f32[8,6,2,512]{0,1,3,2:T(8,128)} %bitcast.114) | data formatting | bytes 393216 | tf_op jit(solution)/shard_map/all_to_all | solution.py:81
  34.5 0.8 %copy.105 = f32[16,6,512]{2,1,0:T(8,128)} copy(f32[16,6,512]{2,0,1:T(8,128)S(1)} %fusion.32) | data formatting | bytes 393216 | tf_op jit(solution)/shard_map/ji,jac->iac/dot_general | solution.py:82
  35.3 4.2 %all-to-all-start.1 = ((f32[16,6,512]{2,1,0:T(8,128)}), f32[16,6,512]{2,1,0:T(8,128)}, u32[]{:S(2)}, u32[]{:S(2)}) async-start(f32[16,6,512]{2,1,0:T(8,128)} %copy.105), calls=%async_computation.1 | async-start | bytes 524288 | tf_op jit(solution)/shard_map/all_to_all | solution.py:83
  39.6 1.1 %convolution_bitcast_fusion.2 = f32[8,6,8,128]{3,2,1,0:T(8,128)} fusion(f32[8,6,8,128]{3,0,2,1:T(8,128)S(1)} %bitcast.119, s32[8]{0:T(128)S(1)} %get-tuple-element.184), kind=kOutput, calls=%fused_computation.35 | convolution fusion | flops 4718720 | bytes 393248 | tf_op jit(solution)/shard_map/tu,iaup->iatp/dot_general | solution.py:90
  40.7 0.7 %mul.90 = f32[8,6,1024]{2,0,1:T(8,128)} reshape(f32[8,6,8,128]{3,2,0,1:T(8,128)S(1)} %copy.102) | data formatting | bytes 393216 | tf_op jit(solution)/shard_map/mul | solution.py:92
  42.1 0.9 %reshape.62 = f32[16,1,3072]{2,1,0:T(1,128)} reshape(f32[16,6,8,64]{3,2,1,0:T(8,128)S(1)} %bitcast.120) | data formatting | bytes 393216
  43.0 2.5 %all-to-all-done.1 = f32[16,6,512]{2,1,0:T(8,128)} async-done(((f32[16,6,512]{2,1,0:T(8,128)}), f32[16,6,512]{2,1,0:T(8,128)}, u32[]{:S(2)}, u32[]{:S(2)}) %all-to-all-start.1) | async-done | bytes 196640 | tf_op jit(solution)/shard_map/all_to_all | solution.py:83
  45.5 6.2 %all-to-all-start.2 = ((f32[16,1,3072]{2,1,0:T(1,128)}), f32[16,1,3072]{2,1,0:T(1,128)S(1)}, u32[]{:S(2)}, u32[]{:S(2)}) async-start(f32[16,1,3072]{2,1,0:T(1,128)} %reshape.62), calls=%async_computation.2 | async-start | bytes 393216 | tf_op jit(solution)/shard_map/all_to_all | solution.py:80
  51.8 3.1 %fusion.28 = (f32[8,6,1024]{2,0,1:T(8,128)}, f32[8,6,1024]{2,0,1:T(8,128)}) fusion(bf16[8,1,6,6,1024]{4,1,3,2,0:T(2,128)(2,1)S(1)} %copy-done.5, f32[8,6,1024]{2,0,1:T(8,128)} %mul.90, f32[8,6,1024]{2,0,1:T(8,128)S(1)} %mul.87, bf16[8,1,6,6,1024]{4,1,3,2,0:T(2,128)(2,1)S(1)} %copy-done.4), kind=kLoop, calls=%fused_computation.25 | loop fusion | flops 1671168 | bytes 1966080 | tf_op jit(solution)/shard_map/reduce_sum | solution.py:92
  55.0 0.5 copy-done.16
  55.6 0.7 %reduce.7 = s32[16,64]{1,0:T(8,128)S(1)} reduce(s32[16,1,64]{2,1,0:T(1,128)S(1)} %copy-done.16, s32[]{:T(128)} %broadcast.31), dimensions={1}, to_apply=%param.23.reduce_sub_computation.3 | reduce | bytes 8196 | tf_op args[9]
  56.4 1.9 %multiply_reduce_fusion = f32[8,6,1024]{2,0,1:T(8,128)} fusion(bf16[8,6,6,1024]{3,0,2,1:T(8,128)(2,1)} %param.16, f32[8,6,1024]{2,0,1:T(8,128)S(1)} %copy-done), kind=kLoop, calls=%fused_computation.32 | loop fusion | flops 835584 | bytes 983040 | tf_op jit(solution)/shard_map/reduce_sum | solution.py:84
  58.2 1.3 %fusion.30 = (f32[8,6,1024]{2,0,1:T(8,128)S(1)}, f32[8,6,1024]{2,0,1:T(8,128)S(1)}) fusion(bf16[8,1,6,6,1024]{4,1,3,2,0:T(2,128)(2,1)S(1)} %copy-done.2, f32[8,6,1024]{2,0,1:T(8,128)S(1)} %mul.84, f32[8,6,1024]{2,0,1:T(8,128)S(1)} %mul.81, bf16[8,1,6,6,1024]{4,1,3,2,0:T(2,128)(2,1)S(1)} %copy-done.3), kind=kLoop, calls=%fused_computation.29 | loop fusion | flops 1671168 | bytes 1966080 | tf_op jit(solution)/shard_map/reduce_sum | solution.py:92
  59.6 1.1 %copy.149 = f32[2,8,6,512]{3,0,1,2:T(2,128)S(1)} copy(f32[2,8,6,512]{3,2,1,0:T(8,128)} %bitcast.25) | data formatting | bytes 393216 | tf_op jit(solution)/shard_map/all_to_all | solution.py:83
  60.9 1.1 %reduce.8 = f32[16,3072]{1,0:T(8,128)S(1)} reduce(f32[16,1,3072]{2,1,0:T(1,128)S(1)} %all-to-all-done.2, f32[]{:T(128)} %broadcast.33), dimensions={1}, to_apply=%all_to_all.37.reduce_sub_computation | reduce | bytes 393220 | tf_op jit(solution)/shard_map/all_to_all | solution.py:80
  62.5 3.4 %while.26 = (s32[]{:T(128)}, f32[48,1024]{1,0:T(8,128)S(1)}, f32[48,1024]{1,0:T(8,128)S(1)}, s32[1024]{0:T(1024)S(1)}, s32[]{:T(128)}, /*index=5*/s32[]{:T(128)}, s32[]{:T(128)}, s32[]{:T(128)}) while((s32[]{:T(128)}, f32[48,1024]{1,0:T(8,128)S(1)}, f32[48,1024]{1,0:T(8,128)S(1)}, s32[1024]{0:T(1024)S(1)}, s32[]{:T(128)}, ...), condition=%wide.region_8.9_spmd.clone, body=%wide.region_7.8_spmd.clone.sunk | while | flops 303136768 | bytes 497813 | solution.py:54
  62.6 1.6 %fusion.119 = f32[48,1024]{1,0:T(8,128)S(1)} fusion(s32[512]{0:T(512)S(1)} %dynamic_slice.37, f32[48,1024]{1,0:T(8,128)S(1)} %get-tuple-element.275, f32[48,1024]{1,0:T(8,128)S(1)} %get-tuple-element.284, s32[]{:T(128)S(6)} %select_n.118, pred[]{:T(512)S(6)} %compare.4), kind=kOutput, calls=%fused_computation.16.clone.1 | convolution fusion | flops 303136768 | bytes 493573 | tf_op jit(solution)/shard_map/while/body/eval_jaxpr/dot_general | solution.py:49
  64.3 1.6 %fusion.119 = f32[48,1024]{1,0:T(8,128)S(1)} fusion(s32[512]{0:T(512)S(1)} %dynamic_slice.37, f32[48,1024]{1,0:T(8,128)S(1)} %get-tuple-element.275, f32[48,1024]{1,0:T(8,128)S(1)} %get-tuple-element.284, s32[]{:T(128)S(6)} %select_n.118, pred[]{:T(512)S(6)} %compare.4), kind=kOutput, calls=%fused_computation.16.clone.1 | convolution fusion | flops 303136768 | bytes 493573 | tf_op jit(solution)/shard_map/while/body/eval_jaxpr/dot_general | solution.py:49
  65.9 0.9 %fusion.36 = f32[8,6,1024]{2,0,1:T(8,128)} fusion(f32[8,6,1024]{2,0,1:T(8,128)S(1)} %copy-done, f32[8,6,1024]{2,0,1:T(8,128)S(1)} %copy-done.13, f32[8,6,1024]{2,1,0:T(8,128)S(1)} %reshape.36, f32[8,6,1024]{2,0,1:T(8,128)S(1)} %all_to_all.36, f32[8,6,1024]{2,0,1:T(8,128)S(1)} %copy-done.10, f32[8,6,1024]{2,0,1:T(8,128)S(1)} %copy-done.8, ...), kind=kLoop, calls=%fused_computation.46 | loop fusion | flops 442368 | bytes 1970176 | tf_op jit(solution)/shard_map/sub | solution.py:97
  (79 shorter events, 3.5 us)
Async XLA Ops:
  3.4 8.0 %copy-start = (f32[8,6,1024]{2,0,1:T(8,128)S(1)}, f32[8,6,1024]{2,0,1:T(8,128)}, u32[]{:S(2)}) copy-start(f32[8,6,1024]{2,0,1:T(8,128)} %param.14) | copy-start | bytes 589828
  3.4 8.1 %copy-start.18 = (s32[8,4]{0,1:T(4,128)S(1)}, s32[8,4]{0,1:T(4,128)}, u32[]{:S(2)}) copy-start(s32[8,4]{0,1:T(4,128)} %param.18) | copy-start | bytes 388
  3.4 8.9 %copy-start.1 = (bf16[8,4,6,6,1024]{4,1,3,2,0:T(4,128)(2,1)S(1)}, bf16[8,4,6,6,1024]{4,1,3,2,0:T(4,128)(2,1)}, u32[]{:S(2)}) copy-start(bf16[8,4,6,6,1024]{4,1,3,2,0:T(4,128)(2,1)} %param.17) | copy-start | bytes 7077892
  7.2 18.7 %all-to-all-start = ((f32[2,1,24576]{2,1,0:T(1,128)}), f32[2,1,24576]{2,1,0:T(1,128)S(1)}, u32[]{:S(2)}, u32[]{:S(2)}) async-start(f32[2,1,24576]{2,1,0:T(1,128)} %reshape.64), calls=%async_computation | async-start | bytes 393216 | tf_op jit(solution)/shard_map/all_to_all | solution.py:81
  12.3 6.8 %copy-start.19 = (s32[1,16]{1,0:T(1,128)S(1)}, s32[1,16]{1,0:T(1,128)}, u32[]{:S(2)}) copy-start(s32[1,16]{1,0:T(1,128)} %param.22) | copy-start | bytes 196
  12.4 7.8 %copy-start.14 = (f32[1,16,64]{2,1,0:T(8,128)S(1)}, f32[1,16,64]{2,1,0:T(8,128)}, u32[]{:S(2)}) copy-start(f32[1,16,64]{2,1,0:T(8,128)} %param.21) | copy-start | bytes 12292
  12.4 7.9 %copy-start.15 = (s32[1,16,64]{2,1,0:T(8,128)S(1)}, s32[1,16,64]{2,1,0:T(8,128)}, u32[]{:S(2)}) copy-start(s32[1,16,64]{2,1,0:T(8,128)} %param.20) | copy-start | bytes 12292
  35.3 6.1 %copy-start.12 = (f32[2,48,512]{2,1,0:T(8,128)S(1)}, f32[2,48,512]{2,1,0:T(8,128)}, u32[]{:S(2)}) copy-start(f32[2,48,512]{2,1,0:T(8,128)} %get-tuple-element.131) | copy-start | bytes 589828
  35.3 10.2 %all-to-all-start.1 = ((f32[16,6,512]{2,1,0:T(8,128)}), f32[16,6,512]{2,1,0:T(8,128)}, u32[]{:S(2)}, u32[]{:S(2)}) async-start(f32[16,6,512]{2,1,0:T(8,128)} %copy.105), calls=%async_computation.1 | async-start | bytes 524288 | tf_op jit(solution)/shard_map/all_to_all | solution.py:83
  41.6 10.2 %copy-start.4 = (bf16[8,1,6,6,1024]{4,1,3,2,0:T(2,128)(2,1)S(1)}, bf16[8,1,6,6,1024]{4,1,3,2,0:T(2,128)(2,1)}, u32[]{:S(2)}) copy-start(bf16[8,1,6,6,1024]{4,1,3,2,0:T(2,128)(2,1)} %get-tuple-element.181) | copy-start | bytes 1769476
  41.6 10.2 %copy-start.5 = (bf16[8,1,6,6,1024]{4,1,3,2,0:T(2,128)(2,1)S(1)}, bf16[8,1,6,6,1024]{4,1,3,2,0:T(2,128)(2,1)}, u32[]{:S(2)}) copy-start(bf16[8,1,6,6,1024]{4,1,3,2,0:T(2,128)(2,1)} %get-tuple-element.183) | copy-start | bytes 1769476
  45.5 15.3 %all-to-all-start.2 = ((f32[16,1,3072]{2,1,0:T(1,128)}), f32[16,1,3072]{2,1,0:T(1,128)S(1)}, u32[]{:S(2)}, u32[]{:S(2)}) async-start(f32[16,1,3072]{2,1,0:T(1,128)} %reshape.62), calls=%async_computation.2 | async-start | bytes 393216 | tf_op jit(solution)/shard_map/all_to_all | solution.py:80
  51.8 3.1 %copy-start.6 = (f32[8,6,8,128]{3,2,1,0:T(8,128)S(1)}, f32[8,6,8,128]{3,2,1,0:T(8,128)}, u32[]{:S(2)}) copy-start(f32[8,6,8,128]{3,2,1,0:T(8,128)} %convolution_bitcast_fusion.3) | copy-start | bytes 589828
  51.8 3.2 %copy-start.7 = (f32[8,6,8,128]{3,2,1,0:T(8,128)S(1)}, f32[8,6,8,128]{3,2,1,0:T(8,128)}, u32[]{:S(2)}) copy-start(f32[8,6,8,128]{3,2,1,0:T(8,128)} %convolution_bitcast_fusion.2) | copy-start | bytes 589828
  54.9 0.7 %copy-start.16 = (s32[16,1,64]{2,1,0:T(1,128)S(1)}, s32[16,1,64]{2,1,0:T(1,128)}, u32[]{:S(2)}) copy-start(s32[16,1,64]{2,1,0:T(1,128)} %param.23) | copy-start | bytes 12292
  54.9 3.4 %copy-start.3 = (bf16[8,1,6,6,1024]{4,1,3,2,0:T(2,128)(2,1)S(1)}, bf16[8,1,6,6,1024]{4,1,3,2,0:T(2,128)(2,1)}, u32[]{:S(2)}) copy-start(bf16[8,1,6,6,1024]{4,1,3,2,0:T(2,128)(2,1)} %get-tuple-element.182) | copy-start | bytes 1769476
  54.9 3.4 %copy-start.2 = (bf16[8,1,6,6,1024]{4,1,3,2,0:T(2,128)(2,1)S(1)}, bf16[8,1,6,6,1024]{4,1,3,2,0:T(2,128)(2,1)}, u32[]{:S(2)}) copy-start(bf16[8,1,6,6,1024]{4,1,3,2,0:T(2,128)(2,1)} %get-tuple-element.180) | copy-start | bytes 1769476
  60.9 1.6 %copy-start.11 = (f32[48,1024]{1,0:T(8,128)S(1)}, f32[48,1024]{1,0:T(8,128)}, u32[]{:S(2)}) copy-start(f32[48,1024]{1,0:T(8,128)} %custom-call) | copy-start | bytes 589828
  62.4 3.5 %copy-start.8 = (f32[8,6,1024]{2,0,1:T(8,128)S(1)}, f32[8,6,1024]{2,0,1:T(8,128)}, u32[]{:S(2)}) copy-start(f32[8,6,1024]{2,0,1:T(8,128)} %get-tuple-element.188) | copy-start | bytes 589828
  62.4 3.5 %copy-start.9 = (f32[8,6,1024]{2,0,1:T(8,128)S(1)}, f32[8,6,1024]{2,0,1:T(8,128)}, u32[]{:S(2)}) copy-start(f32[8,6,1024]{2,0,1:T(8,128)} %get-tuple-element.189) | copy-start | bytes 589828
  62.4 3.5 %copy-start.10 = (f32[8,6,1024]{2,0,1:T(8,128)S(1)}, f32[8,6,1024]{2,0,1:T(8,128)}, u32[]{:S(2)}) copy-start(f32[8,6,1024]{2,0,1:T(8,128)} %multiply_reduce_fusion) | copy-start | bytes 589828
  62.5 3.5 %copy-start.13 = (f32[8,6,1024]{2,0,1:T(8,128)S(1)}, f32[8,6,1024]{2,0,1:T(8,128)}, u32[]{:S(2)}) copy-start(f32[8,6,1024]{2,0,1:T(8,128)} %param.15) | copy-start | bytes 589828
  62.5 3.5 %copy-start.17 = (f32[1024]{0:T(1024)S(1)}, f32[1024]{0:T(1024)}, u32[]{:S(2)}) copy-start(f32[1024]{0:T(1024)} %param.19) | copy-start | bytes 12292
where the time goes:
time: 67.4 us; the launch traced here: 66.9 us
  local copies, waits for them, and re-layouts  27.5 us (41%)
  starting transfers between devices  14.6 us (22%)
  other arithmetic  11 us (16%)
  matrix products  10.8 us (16%)
  waiting for transfers between devices  2.54 us (4%)
    unnamed x47, local copies, waits for them, and re-layouts  13.4 us
    slice x1, local copies, waits for them, and re-layouts, on_device(): jac_face[:, face].astype(jnp.float32) * near[:, :, None, :]  6.2 us
    all_to_all x1, starting transfers between devices, on_device(): lax.all_to_all(outgoing, 'cell', split_axis=2, concat_axis=2, tiled=True)  6.19 us
    reduce_sum x2, other arithmetic, on_device(): jnp.sum(jac_face[:, face].astype(jnp.float32) * near[:, :, None, :], axis=1)  4.4 us
    dot_general x2, matrix products, one_block(): jnp.dot(flat, select, precision=lax.Precision.HIGHEST, preferred_element_...  4.39 us
    all_to_all x1, starting transfers between devices, on_device(): lax.all_to_all(mixed, 'inst', split_axis=0, concat_axis=2, tiled=True)  4.23 us
    all_to_all x1, starting transfers between devices, on_device(): lax.all_to_all(adjoint, 'inst', split_axis=2, concat_axis=0, tiled=True)  4.21 us
    dot_general x2, matrix products, add_block(): jnp.dot(value_block, select, precision=lax.Precision.HIGHEST, preferred_e...  3.15 us
  transfers between devices with their start and end apart: 3, of which 1 were waited for; matrix products, arithmetic and copies ran while one was open for 39% of the time, Pallas kernels for 0%

commit v1 on v0

--- a/solution.py
+++ b/solution.py
@@ -1,13 +1,20 @@
+import functools
 import math
 
 import jax
 import jax.numpy as jnp
+import ml_dtypes
+import numpy as np
 from jax import lax
+from jax.experimental import pallas as pl
+from jax.experimental.pallas import tpu as pltpu
 from jax.sharding import PartitionSpec as P
 
 INSTANCES = 16
 FACES = 4
 TILE = 128
+VARS = 6
+MESH = pl.DeviceIdType.MESH
 
 
 def spectral_matrix(count):
@@ -97,6 +104,326 @@
     return adjoint - dtau[None, None, :] * total
 
 
+def spectral_blocks(inst_count, inst_dev):
+    offset = np.arange(INSTANCES)[:, None] - np.arange(INSTANCES)[None, :]
+    angle = offset * (np.pi / INSTANCES)
+    parity = np.where(offset % 2 == 0, 1.0, -1.0)
+    denom = np.where(offset == 0, 1.0, np.sin(angle))
+    smat = np.where(offset == 0, 0.0, 0.25 * parity * np.cos(angle) / denom).astype(np.float32)
+    high = smat.astype(ml_dtypes.bfloat16)
+    low = (smat - high.astype(np.float32)).astype(ml_dtypes.bfloat16)
+    blocks = []
+    for me in range(inst_count):
+        for hop in range(inst_count):
+            other = (me - hop) % inst_count
+            rows = []
+            for part in (high, low):
+                cut = part[other * inst_dev : (other + 1) * inst_dev, me * inst_dev : (me + 1) * inst_dev]
+                wide = np.kron(np.eye(VARS, dtype=np.float32), cut.T.astype(np.float32))
+                rows.append(np.concatenate([wide, wide], axis=1))
+            blocks.append(np.concatenate(rows, axis=0))
+    side = 2 * VARS * inst_dev
+    stacked = np.stack(blocks).reshape(inst_count, inst_count, side, side)
+    return jnp.asarray(stacked.astype(ml_dtypes.bfloat16))
+
+
+def split_parts(value):
+    high = value.astype(jnp.bfloat16)
+    low = (value - high.astype(jnp.float32)).astype(jnp.bfloat16)
+    return high, low
+
+
+def step_kernel(
+    ninst,
+    npeer,
+    adj_hbm,
+    src_hbm,
+    diag_hbm,
+    face_hbm,
+    nbr_ref,
+    dtau_ref,
+    fsrc_ref,
+    fwt_ref,
+    cnt_ref,
+    fdst_ref,
+    spec_ref,
+    out_ref,
+    adj,
+    source,
+    diag,
+    facej,
+    parts,
+    far,
+    far_parts,
+    near,
+    faced,
+    total,
+    slots,
+    coefs,
+    packs,
+    landed,
+    values,
+    place,
+    load_sem,
+    far_send,
+    far_recv,
+    fr_send,
+    fr_recv,
+):
+    rows, cells = adj.shape
+    idev = rows // VARS
+    tiles = cells // TILE
+    half = rows // 2
+    pairs = npeer // 2
+    cap = TILE // 2
+    strip = tiles * FACES
+    my_inst = lax.axis_index("inst")
+    my_cell = lax.axis_index("cell")
+
+    loads = [
+        pltpu.make_async_copy(adj_hbm, adj, load_sem.at[0]),
+        pltpu.make_async_copy(face_hbm, facej, load_sem.at[1]),
+        pltpu.make_async_copy(diag_hbm, diag, load_sem.at[2]),
+        pltpu.make_async_copy(src_hbm, source, load_sem.at[3]),
+    ]
+    for load in loads:
+        load.start()
+
+    barrier = pltpu.get_barrier_semaphore()
+    for hop in range(1, ninst):
+        pl.semaphore_signal(
+            barrier, inc=1, device_id=(lax.rem(my_inst + hop, ninst), my_cell), device_id_type=MESH
+        )
+    for hop in range(1, npeer):
+        pl.semaphore_signal(
+            barrier, inc=1, device_id=(my_inst, lax.rem(my_cell + hop, npeer)), device_id_type=MESH
+        )
+
+    lane = lax.broadcasted_iota(jnp.int32, (1, TILE), 1)
+    low_half = lane < cap
+    slots[...] = jnp.concatenate([fsrc_ref[0:pairs, :], fsrc_ref[pairs:npeer, :]], axis=1)
+    coefs[...] = jnp.concatenate([fwt_ref[0:pairs, :], fwt_ref[pairs:npeer, :]], axis=1)
+    loads[0].wait()
+    high, low = split_parts(adj[...])
+    parts[0:rows, :] = high
+    parts[rows:, :] = low
+
+    pl.semaphore_wait(barrier, ninst + npeer - 2)
+    far_copies = []
+    for hop in range(1, ninst):
+        copy = pltpu.make_async_remote_copy(
+            src_ref=adj,
+            dst_ref=far.at[hop - 1],
+            send_sem=far_send.at[hop - 1],
+            recv_sem=far_recv.at[hop - 1],
+            device_id=(lax.rem(my_inst + hop, ninst), my_cell),
+            device_id_type=MESH,
+        )
+        copy.start()
+        far_copies.append(copy)
+
+    def fringe_copy(peer, hop):
+        return pltpu.make_async_remote_copy(
+            src_ref=packs.at[peer],
+            dst_ref=landed.at[my_cell],
+            send_sem=fr_send.at[hop],
+            recv_sem=fr_recv.at[hop],
+            device_id=(my_inst, peer),
+            device_id_type=MESH,
+        )
+
+    cell_rows = lax.broadcasted_iota(jnp.int32, (cells, 2 * TILE), 0)
+    wide_low = jnp.broadcast_to(low_half, (half, TILE))
+    place_of = lax.rem(lane, cap)
+    steps = pairs // 2
+    for step in range(steps):
+        first = 2 * lax.rem(my_cell // 2 + step, steps)
+        picked_slots = jnp.concatenate(
+            [slots[pl.ds(first, 1), :], slots[pl.ds(first + 1, 1), :]], axis=1
+        )
+        select = jnp.where(cell_rows == picked_slots, 1.0, 0.0).astype(jnp.bfloat16)
+        both = jnp.dot(parts[...], select, preferred_element_type=jnp.float32)
+        picked = both[0:rows, :] + both[rows:, :]
+        for sub in range(2):
+            pair = first + sub
+            live = place_of < jnp.where(low_half, cnt_ref[0, pair], cnt_ref[0, pair + pairs])
+            coef = jnp.where(live, coefs[pl.ds(pair, 1), :], 0.0)
+            block = picked[:, sub * TILE : (sub + 1) * TILE] * coef
+            upper, lower = block[0:half, :], block[half:, :]
+            packs[pair] = jnp.where(wide_low, upper, pltpu.roll(lower, cap, 1))
+            packs[pair + pairs] = jnp.where(wide_low, pltpu.roll(upper, cap, 1), lower)
+            for peer in (pair, pair + pairs):
+                hop = lax.rem(peer - my_cell + npeer, npeer)
+
+                @pl.when(hop != 0)
+                def _():
+                    fringe_copy(peer, hop).start()
+
+    landed[my_cell] = packs[my_cell]
+
+    for tile in range(tiles):
+        for face in range(FACES):
+            other = nbr_ref[face, tile]
+            for var in range(VARS):
+                span = slice(var * idev, (var + 1) * idev)
+                value = adj[span, 0:TILE]
+                for cand in range(1, tiles):
+                    value = jnp.where(other == cand, adj[span, cand * TILE : (cand + 1) * TILE], value)
+                at = var * idev * strip + tile * FACES + face
+                near[pl.ds(at, idev, stride=strip), :] = value
+
+    cell_ids = lax.broadcasted_iota(jnp.int32, (cells, TILE), 0)
+    for pair in range(pairs):
+        donors = jnp.concatenate([fdst_ref[pair], fdst_ref[pair + pairs]], axis=1)
+        hit = jnp.where(cell_ids == donors, 1.0, 0.0).astype(jnp.bfloat16)
+        place[:, pair * TILE : (pair + 1) * TILE] = hit
+
+    loads[1].wait()
+
+    def one_instance(inst, carry):
+        sums = [jnp.zeros((strip, TILE), jnp.float32) for _ in range(VARS)]
+        for var in range(VARS):
+            start = pl.multiple_of((var * idev + inst) * strip, strip)
+            beside = near[pl.ds(start, strip), :]
+            for eqn in range(VARS):
+                sums[eqn] = sums[eqn] + facej[inst, var, eqn].astype(jnp.float32) * beside
+        for eqn in range(VARS):
+            start = pl.multiple_of((eqn * idev + inst) * strip, strip)
+            faced[pl.ds(start, strip), :] = sums[eqn]
+        return carry
+
+    lax.fori_loop(0, idev, one_instance, 0)
+
+    both = jnp.dot(spec_ref[my_inst, 0], parts[...], preferred_element_type=jnp.float32)
+    total[...] = both[0:rows, :] + both[rows:, :]
+    loads[2].wait()
+    loads[3].wait()
+    for tile in range(tiles):
+        cols = slice(tile * TILE, (tile + 1) * TILE)
+        mine = [adj[var * idev : (var + 1) * idev, cols] for var in range(VARS)]
+        for eqn in range(VARS):
+            span = slice(eqn * idev, (eqn + 1) * idev)
+            value = total[span, cols] - source[span, cols]
+            for var in range(VARS):
+                value = value + diag[var, eqn, :, cols].astype(jnp.float32) * mine[var]
+            for face in range(FACES):
+                at = eqn * idev * strip + tile * FACES + face
+                value = value + faced[pl.ds(at, idev, stride=strip), :]
+            total[span, cols] = value
+
+    for hop in range(1, ninst):
+        far_copies[hop - 1].wait_recv()
+        high, low = split_parts(far[hop - 1])
+        far_parts[0:rows, :] = high
+        far_parts[rows:, :] = low
+        both = jnp.dot(spec_ref[my_inst, hop], far_parts[...], preferred_element_type=jnp.float32)
+        total[...] += both[0:rows, :] + both[rows:, :]
+
+    for hop in range(1, npeer):
+        fringe_copy(lax.rem(my_cell + hop, npeer), hop).wait_recv()
+    for pair in range(pairs):
+        one, two = landed[pair], landed[pair + pairs]
+        cols = slice(pair * TILE, (pair + 1) * TILE)
+        high, low = split_parts(jnp.where(wide_low, one, pltpu.roll(two, cap, 1)))
+        values[0:half, cols] = high
+        values[rows : rows + half, cols] = low
+        high, low = split_parts(jnp.where(wide_low, pltpu.roll(one, cap, 1), two))
+        values[half:rows, cols] = high
+        values[rows + half :, cols] = low
+    for chunk in range(cells // 256):
+        both = lax.dot_general(
+            values[...],
+            place[chunk * 256 : (chunk + 1) * 256, :],
+            (((1,), (1,)), ((), ())),
+            preferred_element_type=jnp.float32,
+        )
+        fringe = both[0:rows, :] + both[rows:, :]
+        for sub in range(2):
+            tile = chunk * 2 + sub
+            cols = slice(tile * TILE, (tile + 1) * TILE)
+            whole = total[:, cols] + fringe[:, sub * TILE : (sub + 1) * TILE]
+            out_ref[:, cols] = adj[:, cols] - dtau_ref[tile : tile + 1, :] * whole
+
+    for copy in far_copies:
+        copy.wait_send()
+    for hop in range(1, npeer):
+        fringe_copy(lax.rem(my_cell + hop, npeer), hop).wait_send()
+
+
+def fused_step(
+    ninst,
+    npeer,
+    adjoint,
+    source,
+    jac_diag,
+    jac_face,
+    tile_nbr,
+    dtau,
+    fringe_src,
+    fringe_wt,
+    fringe_count,
+    fringe_dst,
+):
+    idev, nvars, cells = adjoint.shape
+    tiles = cells // TILE
+    rows = idev * nvars
+    pairs = npeer // 2
+    strip = tiles * FACES
+    adj = jnp.transpose(adjoint, (1, 0, 2)).reshape(rows, cells)
+    src = jnp.transpose(source, (1, 0, 2)).reshape(rows, cells)
+    diag = jnp.transpose(jac_diag, (1, 2, 0, 3))
+    face = jac_face.reshape(idev, FACES, nvars, nvars, tiles, TILE)
+    face = jnp.transpose(face, (0, 2, 3, 4, 1, 5)).reshape(idev, nvars, nvars, strip, TILE)
+    anywhere = pl.BlockSpec(memory_space=pltpu.HBM)
+    vmem = pl.BlockSpec(memory_space=pltpu.VMEM)
+    smem = pl.BlockSpec(memory_space=pltpu.SMEM)
+    out = pl.pallas_call(
+        functools.partial(step_kernel, ninst, npeer),
+        out_shape=jax.ShapeDtypeStruct((rows, cells), jnp.float32),
+        in_specs=[anywhere] * 4 + [smem, vmem, vmem, vmem, smem, vmem, vmem],
+        out_specs=vmem,
+        scratch_shapes=[
+            pltpu.VMEM((rows, cells), jnp.float32),
+            pltpu.VMEM((rows, cells), jnp.float32),
+            pltpu.VMEM((nvars, nvars, idev, cells), jnp.bfloat16),
+            pltpu.VMEM((idev, nvars, nvars, strip, TILE), jnp.bfloat16),
+            pltpu.VMEM((2 * rows, cells), jnp.bfloat16),
+            pltpu.VMEM((ninst - 1, rows, cells), jnp.float32),
+            pltpu.VMEM((2 * rows, cells), jnp.bfloat16),
+            pltpu.VMEM((rows * strip, TILE), jnp.float32),
+            pltpu.VMEM((rows * strip, TILE), jnp.float32),
+            pltpu.VMEM((rows, cells), jnp.float32),
+            pltpu.VMEM((pairs, TILE), jnp.int32),
+            pltpu.VMEM((pairs, TILE), jnp.float32),
+            pltpu.VMEM((npeer, rows // 2, TILE), jnp.float32),
+            pltpu.VMEM((npeer, rows // 2, TILE), jnp.float32),
+            pltpu.VMEM((2 * rows, pairs * TILE), jnp.bfloat16),
+            pltpu.VMEM((cells, pairs * TILE), jnp.bfloat16),
+            pltpu.SemaphoreType.DMA((4,)),
+            pltpu.SemaphoreType.DMA((ninst - 1,)),
+            pltpu.SemaphoreType.DMA((ninst - 1,)),
+            pltpu.SemaphoreType.DMA((npeer,)),
+            pltpu.SemaphoreType.DMA((npeer,)),
+        ],
+        compiler_params=pltpu.CompilerParams(
+            collective_id=0, has_side_effects=True, vmem_limit_bytes=56 * 1024 * 1024
+        ),
+    )(
+        adj,
+        src,
+        diag,
+        face,
+        tile_nbr.T,
+        dtau.reshape(tiles, TILE),
+        fringe_src[0],
+        fringe_wt[0],
+        fringe_count,
+        fringe_dst,
+        spectral_blocks(ninst, idev),
+    )
+    return jnp.transpose(out.reshape(nvars, idev, cells), (1, 0, 2))
+
+
 def solution(mesh):
     placed = (
         P("inst", None, "cell"),
@@ -110,6 +437,16 @@
         P("cell", None),
         P(None, "cell", None),
     )
+    ninst, npeer = mesh.shape["inst"], mesh.shape["cell"]
+
+    def body(adjoint, *rest):
+        idev, _, cells = adjoint.shape
+        slot_cap = rest[5].shape[2]
+        fits = idev % 8 == 0 and ninst > 1 and npeer % 4 == 0
+        if fits and cells % 256 == 0 and slot_cap * 2 == TILE:
+            return fused_step(ninst, npeer, adjoint, *rest)
+        return on_device(adjoint, *rest)
+
     return jax.shard_map(
-        on_device, mesh=mesh, in_specs=placed, out_specs=P("inst", None, "cell"), check_vma=False
+        body, mesh=mesh, in_specs=placed, out_specs=P("inst", None, "cell"), check_vma=False
     )

time: 67.4 us -> 17.4 us (0.26)
  local copies, waits for them, and re-layouts: 27.5 us -> 1.62 us
  Pallas kernels: 0 us -> 15.7 us
  starting transfers between devices: 14.6 us -> 0 us
  other arithmetic: 11 us -> 0 us
  matrix products: 10.8 us -> 0 us
  waiting for transfers between devices: 2.54 us -> 0 us
    pallas_call x0 -> x1, Pallas kernels: none -> 15.7 us  [fused_step(): pl.pallas_call(functools.partial(step_kernel, ninst, npeer), out_shape=ja...]
    all_to_all x3 -> x0, starting transfers between devices: 14.6 us -> none  [the longest x1 6.19 us: on_device(): lax.all_to_all(outgoing, 'cell', split_axis=2, concat_axis=2, tiled=True)]
    unnamed x47 -> x1, local copies, waits for them, and re-layouts: 13.4 us -> 1.62 us
    dot_general x9 -> x0, matrix products: 10.8 us -> none  [the longest x2 4.39 us: one_block(): jnp.dot(flat, select, precision=lax.Precision.HIGHEST, preferred_element_...]
    reduce_sum x3 -> x0, other arithmetic: 6.28 us -> none  [the longest x2 4.4 us: on_device(): jnp.sum(jac_face[:, face].astype(jnp.float32) * near[:, :, None, :], axis=1)]
    slice x1 -> x0, local copies, waits for them, and re-layouts: 6.2 us -> none  [on_device(): jac_face[:, face].astype(jnp.float32) * near[:, :, None, :]]
    all_to_all x5 -> x0, local copies, waits for them, and re-layouts: 4.62 us -> none  [the longest x1 2.65 us: on_device(): lax.all_to_all(adjoint, 'inst', split_axis=2, concat_axis=0, tiled=True)]
    all_to_all x3 -> x0, waiting for transfers between devices: 2.54 us -> none  [the longest x1 2.53 us: on_device(): lax.all_to_all(mixed, 'inst', split_axis=0, concat_axis=2, tiled=True)]
  transfers between devices with their start and end apart: 3 -> 0, of which waited for: 1 -> 0; matrix products, arithmetic and copies ran while one was open for 39% -> 0% of each run, Pallas kernels for 0% -> 0%
where the time goes in v1:
time: 17.4 us; the launch traced here: 17.3 us
  Pallas kernels  15.7 us (90%)
  local copies, waits for them, and re-layouts  1.62 us (9%)
    pallas_call x1, Pallas kernels, fused_step(): pl.pallas_call(functools.partial(step_kernel, ninst, npeer), out_shape=ja...  15.7 us
    unnamed x1, local copies, waits for them, and re-layouts  1.62 us

profile of v1, /device:TPU:0, one launch (start us, length us, event | category | flops | bytes accessed | tf_op | source)
XLA Modules:
  0.0 17.3 jit_solution(2971604868750388969)
XLA Ops:
  0.0 15.7 %shard_map.109 = f32[48,1024]{1,0:T(8,128)} custom-call(f32[48,1024]{1,0:T(8,128)} %bitcast.22, f32[48,1024]{1,0:T(8,128)} %bitcast.23, bf16[6,6,8,1024]{3,2,1,0:T(8,128)(2,1)} %bitcast.21, bf16[8,6,6,32,128]{4,3,2,1,0:T(8,128)(2,1)} %bitcast.19, s32[4,8]{1,0:T(4,128)} %bitcast.27, f32[8,128]{1,0:T(8,128)} %bitcast.26, s32[16,64]{1,0:T(8,128)} %bitcast.24, ...), custom_call_target="tpu_custom_call" | custom-call | tf_op jit(solution)/shard_map/pallas_call | solution.py:380
  15.7 1.6 %copy.14 = f32[8,6,1024]{2,0,1:T(8,128)} copy(f32[8,6,1024]{2,0,1:T(8,128)} %bitcast.20) | data formatting | bytes 393216

commit v2 on v1

--- a/solution.py
+++ b/solution.py
@@ -137,21 +137,28 @@
     ninst,
     npeer,
     adj_hbm,
+    fsrc_hbm,
+    fwt_hbm,
+    cnt_hbm,
+    nbr_hbm,
+    fdst_hbm,
+    face_hbm,
+    diag_hbm,
     src_hbm,
-    diag_hbm,
-    face_hbm,
-    nbr_ref,
-    dtau_ref,
-    fsrc_ref,
-    fwt_ref,
-    cnt_ref,
-    fdst_ref,
-    spec_ref,
+    spec_hbm,
+    dtau_hbm,
     out_ref,
     adj,
+    fsrc,
+    fwt,
+    cnt,
+    nbr,
+    fdst,
+    facej,
+    diag,
     source,
-    diag,
-    facej,
+    spec,
+    dtau,
     parts,
     far,
     far_parts,
@@ -177,18 +184,26 @@
     pairs = npeer // 2
     cap = TILE // 2
     strip = tiles * FACES
+    steps = pairs // 2
     my_inst = lax.axis_index("inst")
     my_cell = lax.axis_index("cell")
 
-    loads = [
-        pltpu.make_async_copy(adj_hbm, adj, load_sem.at[0]),
-        pltpu.make_async_copy(face_hbm, facej, load_sem.at[1]),
-        pltpu.make_async_copy(diag_hbm, diag, load_sem.at[2]),
-        pltpu.make_async_copy(src_hbm, source, load_sem.at[3]),
+    ends = [
+        (adj_hbm, adj),
+        (fsrc_hbm, fsrc),
+        (fwt_hbm, fwt),
+        (cnt_hbm, cnt),
+        (nbr_hbm, nbr),
+        (fdst_hbm, fdst),
+        (face_hbm, facej),
+        (diag_hbm, diag),
+        (src_hbm, source),
+        (spec_hbm.at[my_inst], spec),
+        (dtau_hbm, dtau),
     ]
-    for load in loads:
+    loads = [pltpu.make_async_copy(one, two, load_sem.at[at]) for at, (one, two) in enumerate(ends)]
+    for load in loads[:4]:
         load.start()
-
     barrier = pltpu.get_barrier_semaphore()
     for hop in range(1, ninst):
         pl.semaphore_signal(
@@ -198,16 +213,73 @@
         pl.semaphore_signal(
             barrier, inc=1, device_id=(my_inst, lax.rem(my_cell + hop, npeer)), device_id_type=MESH
         )
-
-    lane = lax.broadcasted_iota(jnp.int32, (1, TILE), 1)
-    low_half = lane < cap
-    slots[...] = jnp.concatenate([fsrc_ref[0:pairs, :], fsrc_ref[pairs:npeer, :]], axis=1)
-    coefs[...] = jnp.concatenate([fwt_ref[0:pairs, :], fwt_ref[pairs:npeer, :]], axis=1)
+    for load in loads[4:]:
+        load.start()
+
+    lane = lax.broadcasted_iota(jnp.int32, (npeer, cap), 1)
+    diagonal = lax.broadcasted_iota(jnp.int32, (npeer, npeer), 0) == lax.broadcasted_iota(
+        jnp.int32, (npeer, npeer), 1
+    )
+    wide_low = lax.broadcasted_iota(jnp.int32, (half, TILE), 1) < cap
+    window = lax.broadcasted_iota(jnp.int32, (256, 256), 0).astype(jnp.float32).astype(jnp.bfloat16)
+    one, zero = jnp.bfloat16(1.0), jnp.bfloat16(0.0)
+
+    def window_hits(ids, at):
+        return jnp.where(window == (ids - 256 * at).astype(jnp.float32).astype(jnp.bfloat16), one, zero)
+
+    for load in loads[1:4]:
+        load.wait()
+    slots[...] = jnp.concatenate([fsrc[0:pairs, :], fsrc[pairs:npeer, :]], axis=1)
+    live_count = jnp.sum(
+        jnp.where(diagonal, jnp.broadcast_to(cnt[...], (npeer, npeer)).astype(jnp.float32), 0.0), axis=1, keepdims=True
+    )
+    coef = jnp.where(lane.astype(jnp.float32) < live_count, fwt[...], 0.0)
+    coefs[...] = jnp.concatenate([coef[0:pairs, :], coef[pairs:npeer, :]], axis=1)
     loads[0].wait()
     high, low = split_parts(adj[...])
     parts[0:rows, :] = high
     parts[rows:, :] = low
 
+    def fringe_copy(peer, hop):
+        return pltpu.make_async_remote_copy(
+            src_ref=packs.at[peer],
+            dst_ref=landed.at[my_cell],
+            send_sem=fr_send.at[hop],
+            recv_sem=fr_recv.at[hop],
+            device_id=(my_inst, peer),
+            device_id_type=MESH,
+        )
+
+    def pick_step(step):
+        first = 2 * lax.rem(my_cell // 2 + step, steps)
+        ids = jnp.concatenate([slots[pl.ds(first, 1), :], slots[pl.ds(first + 1, 1), :]], axis=1)
+        both = jnp.zeros((2 * rows, 256), jnp.float32)
+        for at in range(cells // 256):
+            both = both + jnp.dot(
+                parts[:, at * 256 : (at + 1) * 256],
+                window_hits(ids, at),
+                preferred_element_type=jnp.float32,
+            )
+        picked = both[0:rows, :] + both[rows:, :]
+        for sub in range(2):
+            pair = first + sub
+            block = picked[:, sub * TILE : (sub + 1) * TILE] * coefs[pl.ds(pair, 1), :]
+            upper, lower = block[0:half, :], block[half:, :]
+            packs[pair] = jnp.where(wide_low, upper, pltpu.roll(lower, cap, 1))
+            packs[pair + pairs] = jnp.where(wide_low, pltpu.roll(upper, cap, 1), lower)
+
+    def send_step(step):
+        first = 2 * lax.rem(my_cell // 2 + step, steps)
+        for peer in (first + pairs, first + pairs + 1, first, first + 1):
+            hop = lax.rem(peer - my_cell + npeer, npeer)
+
+            @pl.when(hop != 0)
+            def _():
+                fringe_copy(peer, hop).start()
+
+    early = steps // 2
+    for step in range(early):
+        pick_step(step)
     pl.semaphore_wait(barrier, ninst + npeer - 2)
     far_copies = []
     for hop in range(1, ninst):
@@ -221,64 +293,27 @@
         )
         copy.start()
         far_copies.append(copy)
-
-    def fringe_copy(peer, hop):
-        return pltpu.make_async_remote_copy(
-            src_ref=packs.at[peer],
-            dst_ref=landed.at[my_cell],
-            send_sem=fr_send.at[hop],
-            recv_sem=fr_recv.at[hop],
-            device_id=(my_inst, peer),
-            device_id_type=MESH,
-        )
-
-    cell_rows = lax.broadcasted_iota(jnp.int32, (cells, 2 * TILE), 0)
-    wide_low = jnp.broadcast_to(low_half, (half, TILE))
-    place_of = lax.rem(lane, cap)
-    steps = pairs // 2
-    for step in range(steps):
-        first = 2 * lax.rem(my_cell // 2 + step, steps)
-        picked_slots = jnp.concatenate(
-            [slots[pl.ds(first, 1), :], slots[pl.ds(first + 1, 1), :]], axis=1
-        )
-        select = jnp.where(cell_rows == picked_slots, 1.0, 0.0).astype(jnp.bfloat16)
-        both = jnp.dot(parts[...], select, preferred_element_type=jnp.float32)
-        picked = both[0:rows, :] + both[rows:, :]
-        for sub in range(2):
-            pair = first + sub
-            live = place_of < jnp.where(low_half, cnt_ref[0, pair], cnt_ref[0, pair + pairs])
-            coef = jnp.where(live, coefs[pl.ds(pair, 1), :], 0.0)
-            block = picked[:, sub * TILE : (sub + 1) * TILE] * coef
-            upper, lower = block[0:half, :], block[half:, :]
-            packs[pair] = jnp.where(wide_low, upper, pltpu.roll(lower, cap, 1))
-            packs[pair + pairs] = jnp.where(wide_low, pltpu.roll(upper, cap, 1), lower)
-            for peer in (pair, pair + pairs):
-                hop = lax.rem(peer - my_cell + npeer, npeer)
-
-                @pl.when(hop != 0)
-                def _():
-                    fringe_copy(peer, hop).start()
-
+    for step in range(early):
+        send_step(step)
+    for step in range(early, steps):
+        pick_step(step)
+        send_step(step)
     landed[my_cell] = packs[my_cell]
 
+    loads[4].wait()
     for tile in range(tiles):
         for face in range(FACES):
-            other = nbr_ref[face, tile]
+            other = jnp.broadcast_to(nbr[face : face + 1, tile : tile + 1], (idev, TILE))
+            picks = [other == cand for cand in range(1, tiles)]
             for var in range(VARS):
                 span = slice(var * idev, (var + 1) * idev)
                 value = adj[span, 0:TILE]
                 for cand in range(1, tiles):
-                    value = jnp.where(other == cand, adj[span, cand * TILE : (cand + 1) * TILE], value)
+                    value = jnp.where(picks[cand - 1], adj[span, cand * TILE : (cand + 1) * TILE], value)
                 at = var * idev * strip + tile * FACES + face
                 near[pl.ds(at, idev, stride=strip), :] = value
 
-    cell_ids = lax.broadcasted_iota(jnp.int32, (cells, TILE), 0)
-    for pair in range(pairs):
-        donors = jnp.concatenate([fdst_ref[pair], fdst_ref[pair + pairs]], axis=1)
-        hit = jnp.where(cell_ids == donors, 1.0, 0.0).astype(jnp.bfloat16)
-        place[:, pair * TILE : (pair + 1) * TILE] = hit
-
-    loads[1].wait()
+    loads[6].wait()
 
     def one_instance(inst, carry):
         sums = [jnp.zeros((strip, TILE), jnp.float32) for _ in range(VARS)]
@@ -294,10 +329,10 @@
 
     lax.fori_loop(0, idev, one_instance, 0)
 
-    both = jnp.dot(spec_ref[my_inst, 0], parts[...], preferred_element_type=jnp.float32)
+    for load in loads[7:10]:
+        load.wait()
+    both = jnp.dot(spec[0], parts[...], preferred_element_type=jnp.float32)
     total[...] = both[0:rows, :] + both[rows:, :]
-    loads[2].wait()
-    loads[3].wait()
     for tile in range(tiles):
         cols = slice(tile * TILE, (tile + 1) * TILE)
         mine = [adj[var * idev : (var + 1) * idev, cols] for var in range(VARS)]
@@ -311,38 +346,63 @@
                 value = value + faced[pl.ds(at, idev, stride=strip), :]
             total[span, cols] = value
 
+    loads[5].wait()
+    loads[10].wait()
+    for group in range(steps):
+        pair = 2 * group
+        ids = jnp.concatenate(
+            [fdst[pair], fdst[pair + pairs], fdst[pair + 1], fdst[pair + 1 + pairs]], axis=1
+        )
+        for at in range(cells // 256):
+            place[group, at * 256 : (at + 1) * 256, :] = window_hits(ids, at)
+
+    def take_step(step):
+        group = lax.rem(my_cell // 2 - step + steps, steps)
+        first = 2 * group
+        for origin in (first, first + 1, first + pairs, first + pairs + 1):
+            hop = lax.rem(my_cell - origin + npeer, npeer)
+
+            @pl.when(hop != 0)
+            def _():
+                fringe_copy(lax.rem(my_cell + hop, npeer), hop).wait_recv()
+
+        for sub in range(2):
+            here, there = landed[first + sub], landed[first + sub + pairs]
+            cols = slice(sub * TILE, (sub + 1) * TILE)
+            high, low = split_parts(jnp.where(wide_low, here, pltpu.roll(there, cap, 1)))
+            values[0:half, cols] = high
+            values[rows : rows + half, cols] = low
+            high, low = split_parts(jnp.where(wide_low, pltpu.roll(here, cap, 1), there))
+            values[half:rows, cols] = high
+            values[rows + half :, cols] = low
+        for at in range(cells // 256):
+            both = lax.dot_general(
+                values[...],
+                place[group, at * 256 : (at + 1) * 256, :],
+                (((1,), (1,)), ((), ())),
+                preferred_element_type=jnp.float32,
+            )
+            fringe = both[0:rows, :] + both[rows:, :]
+            for sub in range(2):
+                tile = at * 2 + sub
+                cols = slice(tile * TILE, (tile + 1) * TILE)
+                whole = total[:, cols] + fringe[:, sub * TILE : (sub + 1) * TILE]
+                if step < steps - 1:
+                    total[:, cols] = whole
+                else:
+                    out_ref[:, cols] = adj[:, cols] - dtau[tile : tile + 1, :] * whole
+
+    for step in range(early):
+        take_step(step)
     for hop in range(1, ninst):
         far_copies[hop - 1].wait_recv()
         high, low = split_parts(far[hop - 1])
         far_parts[0:rows, :] = high
         far_parts[rows:, :] = low
-        both = jnp.dot(spec_ref[my_inst, hop], far_parts[...], preferred_element_type=jnp.float32)
+        both = jnp.dot(spec[hop], far_parts[...], preferred_element_type=jnp.float32)
         total[...] += both[0:rows, :] + both[rows:, :]
-
-    for hop in range(1, npeer):
-        fringe_copy(lax.rem(my_cell + hop, npeer), hop).wait_recv()
-    for pair in range(pairs):
-        one, two = landed[pair], landed[pair + pairs]
-        cols = slice(pair * TILE, (pair + 1) * TILE)
-        high, low = split_parts(jnp.where(wide_low, one, pltpu.roll(two, cap, 1)))
-        values[0:half, cols] = high
-        values[rows : rows + half, cols] = low
-        high, low = split_parts(jnp.where(wide_low, pltpu.roll(one, cap, 1), two))
-        values[half:rows, cols] = high
-        values[rows + half :, cols] = low
-    for chunk in range(cells // 256):
-        both = lax.dot_general(
-            values[...],
-            place[chunk * 256 : (chunk + 1) * 256, :],
-            (((1,), (1,)), ((), ())),
-            preferred_element_type=jnp.float32,
-        )
-        fringe = both[0:rows, :] + both[rows:, :]
-        for sub in range(2):
-            tile = chunk * 2 + sub
-            cols = slice(tile * TILE, (tile + 1) * TILE)
-            whole = total[:, cols] + fringe[:, sub * TILE : (sub + 1) * TILE]
-            out_ref[:, cols] = adj[:, cols] - dtau_ref[tile : tile + 1, :] * whole
+    for step in range(early, steps):
+        take_step(step)
 
     for copy in far_copies:
         copy.wait_send()
@@ -374,19 +434,29 @@
     diag = jnp.transpose(jac_diag, (1, 2, 0, 3))
     face = jac_face.reshape(idev, FACES, nvars, nvars, tiles, TILE)
     face = jnp.transpose(face, (0, 2, 3, 4, 1, 5)).reshape(idev, nvars, nvars, strip, TILE)
-    anywhere = pl.BlockSpec(memory_space=pltpu.HBM)
-    vmem = pl.BlockSpec(memory_space=pltpu.VMEM)
-    smem = pl.BlockSpec(memory_space=pltpu.SMEM)
+    spectral = spectral_blocks(ninst, idev)
+    operands = [
+        adj,
+        fringe_src[0],
+        fringe_wt[0],
+        fringe_count,
+        tile_nbr.T,
+        fringe_dst,
+        face,
+        diag,
+        src,
+        spectral,
+        dtau.reshape(tiles, TILE),
+    ]
+    held = [pltpu.VMEM(one.shape, one.dtype) for one in operands]
+    held[9] = pltpu.VMEM(spectral.shape[1:], spectral.dtype)
     out = pl.pallas_call(
         functools.partial(step_kernel, ninst, npeer),
         out_shape=jax.ShapeDtypeStruct((rows, cells), jnp.float32),
-        in_specs=[anywhere] * 4 + [smem, vmem, vmem, vmem, smem, vmem, vmem],
-        out_specs=vmem,
-        scratch_shapes=[
-            pltpu.VMEM((rows, cells), jnp.float32),
-            pltpu.VMEM((rows, cells), jnp.float32),
-            pltpu.VMEM((nvars, nvars, idev, cells), jnp.bfloat16),
-            pltpu.VMEM((idev, nvars, nvars, strip, TILE), jnp.bfloat16),
+        in_specs=[pl.BlockSpec(memory_space=pltpu.HBM)] * len(operands),
+        out_specs=pl.BlockSpec(memory_space=pltpu.VMEM),
+        scratch_shapes=held
+        + [
             pltpu.VMEM((2 * rows, cells), jnp.bfloat16),
             pltpu.VMEM((ninst - 1, rows, cells), jnp.float32),
             pltpu.VMEM((2 * rows, cells), jnp.bfloat16),
@@ -397,9 +467,9 @@
             pltpu.VMEM((pairs, TILE), jnp.float32),
             pltpu.VMEM((npeer, rows // 2, TILE), jnp.float32),
             pltpu.VMEM((npeer, rows // 2, TILE), jnp.float32),
-            pltpu.VMEM((2 * rows, pairs * TILE), jnp.bfloat16),
-            pltpu.VMEM((cells, pairs * TILE), jnp.bfloat16),
-            pltpu.SemaphoreType.DMA((4,)),
+            pltpu.VMEM((2 * rows, 256), jnp.bfloat16),
+            pltpu.VMEM((pairs // 2, cells, 256), jnp.bfloat16),
+            pltpu.SemaphoreType.DMA((len(operands),)),
             pltpu.SemaphoreType.DMA((ninst - 1,)),
             pltpu.SemaphoreType.DMA((ninst - 1,)),
             pltpu.SemaphoreType.DMA((npeer,)),
@@ -408,19 +478,7 @@
         compiler_params=pltpu.CompilerParams(
             collective_id=0, has_side_effects=True, vmem_limit_bytes=56 * 1024 * 1024
         ),
-    )(
-        adj,
-        src,
-        diag,
-        face,
-        tile_nbr.T,
-        dtau.reshape(tiles, TILE),
-        fringe_src[0],
-        fringe_wt[0],
-        fringe_count,
-        fringe_dst,
-        spectral_blocks(ninst, idev),
-    )
+    )(*operands)
     return jnp.transpose(out.reshape(nvars, idev, cells), (1, 0, 2))
 
 

time: 17.4 us -> 16.2 us (0.931)
  Pallas kernels: 15.7 us -> 14.4 us
    pallas_call x1, Pallas kernels: 15.7 us -> 14.4 us  [fused_step(): pl.pallas_call(functools.partial(step_kernel, ninst, npeer), out_shape=ja...]
where the time goes in v2:
time: 16.2 us; the launch traced here: 16 us
  Pallas kernels  14.4 us (89%)
  local copies, waits for them, and re-layouts  1.62 us (10%)
    pallas_call x1, Pallas kernels, fused_step(): pl.pallas_call(functools.partial(step_kernel, ninst, npeer), out_shape=ja...  14.4 us
    unnamed x1, local copies, waits for them, and re-layouts  1.62 us

profile of v2, /device:TPU:0, one launch (start us, length us, event | category | flops | bytes accessed | tf_op | source)
XLA Modules:
  0.0 16.0 jit_solution(2869823147650107972)
XLA Ops:
  0.0 14.4 %shard_map.109 = f32[48,1024]{1,0:T(8,128)} custom-call(f32[48,1024]{1,0:T(8,128)} %bitcast.22, s32[16,64]{1,0:T(8,128)} %bitcast.24, f32[16,64]{1,0:T(8,128)} %bitcast.25, s32[1,16]{1,0:T(1,128)} %cnt_hbm.1, s32[4,8]{1,0:T(4,128)} %bitcast.27, s32[16,1,64]{2,1,0:T(1,128)} %fdst_hbm.1, bf16[8,6,6,32,128]{4,3,2,1,0:T(8,128)(2,1)} %bitcast.19, ...), custom_call_target="tpu_custom_call" | custom-call | tf_op jit(solution)/shard_map/pallas_call | solution.py:453
  14.4 1.6 %copy.14 = f32[8,6,1024]{2,0,1:T(8,128)} copy(f32[8,6,1024]{2,0,1:T(8,128)} %bitcast.20) | data formatting | bytes 393216

commit v3 on v2

--- a/solution.py
+++ b/solution.py
@@ -277,14 +277,14 @@
             def _():
                 fringe_copy(peer, hop).start()
 
-    early = steps // 2
+    early = 1
     for step in range(early):
         pick_step(step)
     pl.semaphore_wait(barrier, ninst + npeer - 2)
     far_copies = []
     for hop in range(1, ninst):
         copy = pltpu.make_async_remote_copy(
-            src_ref=adj,
+            src_ref=adj_hbm,
             dst_ref=far.at[hop - 1],
             send_sem=far_send.at[hop - 1],
             recv_sem=far_recv.at[hop - 1],
@@ -392,7 +392,7 @@
                 else:
                     out_ref[:, cols] = adj[:, cols] - dtau[tile : tile + 1, :] * whole
 
-    for step in range(early):
+    for step in range(steps // 2):
         take_step(step)
     for hop in range(1, ninst):
         far_copies[hop - 1].wait_recv()
@@ -401,13 +401,25 @@
         far_parts[rows:, :] = low
         both = jnp.dot(spec[hop], far_parts[...], preferred_element_type=jnp.float32)
         total[...] += both[0:rows, :] + both[rows:, :]
-    for step in range(early, steps):
+    for step in range(steps // 2, steps):
         take_step(step)
 
     for copy in far_copies:
         copy.wait_send()
     for hop in range(1, npeer):
         fringe_copy(lax.rem(my_cell + hop, npeer), hop).wait_send()
+
+
+def store_kernel(held, out_hbm, sems):
+    span = held.shape[0] // VARS
+    copies = []
+    for var in range(VARS):
+        rows = pl.ds(var * span, span)
+        copies.append(pltpu.make_async_copy(held.at[rows], out_hbm.at[rows], sems.at[var]))
+    for copy in copies:
+        copy.start()
+    for copy in copies:
+        copy.wait()
 
 
 def fused_step(
@@ -452,7 +464,7 @@
     held[9] = pltpu.VMEM(spectral.shape[1:], spectral.dtype)
     out = pl.pallas_call(
         functools.partial(step_kernel, ninst, npeer),
-        out_shape=jax.ShapeDtypeStruct((rows, cells), jnp.float32),
+        out_shape=pltpu.VMEM((rows, cells), jnp.float32),
         in_specs=[pl.BlockSpec(memory_space=pltpu.HBM)] * len(operands),
         out_specs=pl.BlockSpec(memory_space=pltpu.VMEM),
         scratch_shapes=held
@@ -479,6 +491,13 @@
             collective_id=0, has_side_effects=True, vmem_limit_bytes=56 * 1024 * 1024
         ),
     )(*operands)
+    out = pl.pallas_call(
+        store_kernel,
+        out_shape=jax.ShapeDtypeStruct((rows, cells), jnp.float32),
+        in_specs=[pl.BlockSpec(memory_space=pltpu.VMEM)],
+        out_specs=pl.BlockSpec(memory_space=pltpu.HBM),
+        scratch_shapes=[pltpu.SemaphoreType.DMA((nvars,))],
+    )(out)
     return jnp.transpose(out.reshape(nvars, idev, cells), (1, 0, 2))
 
 

time: 16.2 us -> 16.4 us (1.012)
  Pallas kernels: 14.4 us -> 15.6 us
  local copies, waits for them, and re-layouts: 1.62 us -> 0.66 us
    pallas_call x1 -> x2, Pallas kernels: 14.4 us -> 15.6 us  [the longest x1 14 us: fused_step(): pl.pallas_call(functools.partial(step_kernel, ninst, npeer), out_shape=pl...]
    unnamed x1 -> x2, local copies, waits for them, and re-layouts: 1.62 us -> 0.66 us
where the time goes in v3:
time: 16.4 us; the launch traced here: 16.3 us
  Pallas kernels  15.6 us (95%)
  local copies, waits for them, and re-layouts  0.66 us (4%)
    pallas_call x1, Pallas kernels, fused_step(): pl.pallas_call(functools.partial(step_kernel, ninst, npeer), out_shape=pl...  14 us
    pallas_call x1, Pallas kernels, fused_step(): pl.pallas_call(store_kernel, out_shape=jax.ShapeDtypeStruct((rows, cells)...  1.65 us
    unnamed x2, local copies, waits for them, and re-layouts  0.66 us

profile of v3, /device:TPU:0, one launch (start us, length us, event | category | flops | bytes accessed | tf_op | source)
XLA Modules:
  0.0 16.3 jit_solution(14549432266645580439)
XLA Ops:
  0.0 14.0 %shard_map.109.held = f32[48,1024]{1,0:T(8,128)S(1)} custom-call(f32[48,1024]{1,0:T(8,128)} %bitcast.21, s32[16,64]{1,0:T(8,128)} %bitcast.23, f32[16,64]{1,0:T(8,128)} %bitcast.24, s32[1,16]{1,0:T(1,128)} %cnt_hbm.1, s32[4,8]{1,0:T(4,128)} %bitcast.26, s32[16,1,64]{2,1,0:T(1,128)} %fdst_hbm.1, bf16[8,6,6,32,128]{4,3,2,1,0:T(8,128)(2,1)} %bitcast.19, ...), custom_call_target="tpu_custom_call" | custom-call | tf_op jit(solution)/shard_map/pallas_call | solution.py:465
  14.0 0.0 copy-start
  14.0 0.7 %copy-done = f32[48,1024]{1,0:T(8,128)} copy-done((f32[48,1024]{1,0:T(8,128)}, f32[48,1024]{1,0:T(8,128)S(1)}, u32[]{:S(2)}) %copy-start) | copy-done | bytes 196632
  14.6 1.6 %shard_map.110 = f32[48,1024]{1,0:T(8,128)} custom-call(f32[48,1024]{1,0:T(8,128)} %copy-done), custom_call_target="tpu_custom_call" | custom-call | tf_op jit(solution)/shard_map/pallas_call | solution.py:494
Async XLA Ops:
  14.0 0.7 %copy-start = (f32[48,1024]{1,0:T(8,128)}, f32[48,1024]{1,0:T(8,128)S(1)}, u32[]{:S(2)}) copy-start(f32[48,1024]{1,0:T(8,128)S(1)} %shard_map.109.held) | copy-start | bytes 589828

commit v4 on v3

--- a/solution.py
+++ b/solution.py
@@ -497,6 +497,7 @@
         in_specs=[pl.BlockSpec(memory_space=pltpu.VMEM)],
         out_specs=pl.BlockSpec(memory_space=pltpu.HBM),
         scratch_shapes=[pltpu.SemaphoreType.DMA((nvars,))],
+        compiler_params=pltpu.CompilerParams(vmem_limit_bytes=1024 * 1024),
     )(out)
     return jnp.transpose(out.reshape(nvars, idev, cells), (1, 0, 2))
 

time: 16.4 us -> 14.8 us (0.902)
  Pallas kernels: 15.6 us -> 14.7 us
  local copies, waits for them, and re-layouts: 0.66 us -> 0 us
    pallas_call x1, Pallas kernels: 1.65 us -> 0.72 us  [fused_step(): pl.pallas_call(store_kernel, out_shape=jax.ShapeDtypeStruct((rows, cells)...]
    unnamed x2 -> x0, local copies, waits for them, and re-layouts: 0.66 us -> none
where the time goes in v4:
time: 14.8 us; the launch traced here: 14.7 us
  Pallas kernels  14.7 us (99%)
    pallas_call x1, Pallas kernels, fused_step(): pl.pallas_call(functools.partial(step_kernel, ninst, npeer), out_shape=pl...  14 us
    pallas_call x1, Pallas kernels, fused_step(): pl.pallas_call(store_kernel, out_shape=jax.ShapeDtypeStruct((rows, cells)...  0.72 us

profile of v4, /device:TPU:0, one launch (start us, length us, event | category | flops | bytes accessed | tf_op | source)
XLA Modules:
  0.0 14.7 jit_solution(14270738553189323833)
XLA Ops:
  0.0 14.0 %shard_map.109.held = f32[48,1024]{1,0:T(8,128)S(1)} custom-call(f32[48,1024]{1,0:T(8,128)} %bitcast.21, s32[16,64]{1,0:T(8,128)} %bitcast.23, f32[16,64]{1,0:T(8,128)} %bitcast.24, s32[1,16]{1,0:T(1,128)} %cnt_hbm.1, s32[4,8]{1,0:T(4,128)} %bitcast.26, s32[16,1,64]{2,1,0:T(1,128)} %fdst_hbm.1, bf16[8,6,6,32,128]{4,3,2,1,0:T(8,128)(2,1)} %bitcast.19, ...), custom_call_target="tpu_custom_call" | custom-call | tf_op jit(solution)/shard_map/pallas_call | solution.py:465
  14.0 0.7 %shard_map.110 = f32[48,1024]{1,0:T(8,128)} custom-call(f32[48,1024]{1,0:T(8,128)S(1)} %shard_map.109.held), custom_call_target="tpu_custom_call" | custom-call | tf_op jit(solution)/shard_map/pallas_call | solution.py:494
